TPU v7x, 32 devices: a whole 2x2x4 slice. The times are simulated.
32 devices in a mesh: grow: 8 (over z, x), wide: 4 (over y, core).
Axes of the slice: x: 2, y: 2, z: 4, core: 2. Of those that a mesh axis runs over, the one named last changes fastest.
Arguments:
- fields: float32 [3, 128, 128, 128], P(None, 'grow', 'wide'), may hold values from -1 to 1
- melt_planes: float32 [3, 16, 128, 128], P(None, None, 'wide'), may hold values from -1 to 1
- slide_planes: int32 [8], replicated, may hold values from 0 to 8, as said below
Outputs:
- evolved: float32 [3, 128, 128, 128], P(None, 'grow', 'wide')
Inputs may be any that keep to these rules, and one draw needn't show every extreme that they name: `slide_planes`: entries at even positions k are 0; at least one entry equals 8, and at most one other entry is nonzero.
All inputs are finite; a program needn't handle non-finite values.
Results may differ from a plain program's by a relative error of at most 0.0001.
Values sent between devices are 32-bit elements; how exact they have to be, the bound alone decides.
No kernel may reach another device: no remote copies, remote signals or barrier semaphores. Data moves between devices by JAX's collectives and lax.ppermute only.
A program may use at most 64 MiB of HBM per device.

v0:
```python
import functools

import jax
import jax.numpy as jnp
from jax import lax
from jax.experimental import pallas as pl
from jax.experimental.pallas import tpu as pltpu
from jax.sharding import PartitionSpec as P

TILE = 8
EARLY, MIDDLE, LATE = 0, 1, 2
GROUPS = ((6,), (16,), (8, 4, 2))
PIECES = 2
MIDDLE_FLOPS = 3_500_000_000

coef_phase = 0.15
coef_react = 0.3
coef_couple = 0.4
coef_solute = 1.5
coef_diff = 0.1
coef_heat = 0.16


def passed(value, grow_step, wide_pairs=None):
    grow, wide = lax.axis_size("grow"), lax.axis_size("wide")
    if wide_pairs is None:
        return lax.ppermute(value, "grow", [(g, g + grow_step) for g in range(grow) if 0 <= g + grow_step < grow])
    lanes = wide_pairs + [(b, a) for a, b in wide_pairs]
    if grow_step == 0:
        return lax.ppermute(value, "wide", lanes)
    pairs = [
        (g * wide + a, (g + grow_step) * wide + b)
        for g in range(grow)
        if 0 <= g + grow_step < grow
        for a, b in lanes
    ]
    return lax.ppermute(value, ("grow", "wide"), pairs)


def stage_kernel(stage, rows, cols, slide_rows, *refs):
    *refs, slide_ref = refs
    steps = slide_ref.shape[0]
    reach = steps
    count = rows + 2 * reach
    zero_slot = count + 2 * reach
    first_col = 2 * TILE
    first_row = first_col - reach
    tiles = cols // TILE + 2 * (reach // TILE)
    total_rows = rows * lax.axis_size("grow")
    grow_index, wide_index = lax.axis_index("grow"), lax.axis_index("wide")
    at_end = grow_index == lax.axis_size("grow") - 1
    next_end = grow_index == lax.axis_size("grow") - 2
    is_even = lax.rem(wide_index, 2) == 0
    low_inside = wide_index > 0
    high_inside = wide_index < lax.axis_size("wide") - 1

    slides = slide_rows[...]
    total = jnp.int32(0)
    for k in range(steps):
        shift = slides[k, 0]
        slide_ref[k] = shift
        total = total + shift
    extra = total - reach
    base = grow_index * rows + extra - reach
    low_col, high_col = first_row, first_col + cols
    outer_col = pl.multiple_of(jnp.where(is_even, low_col, high_col), TILE)
    inner_col = pl.multiple_of(jnp.where(is_even, high_col, low_col), TILE)

    if stage == EARLY:
        own, outer_both, inner_both, even, odd, token, sems = refs
    elif stage == MIDDLE:
        near, melt, outer_both, inner_both, outer_near, *inner_near, _, _, even, odd, token, sems = refs
    else:
        far, melt, outer_both, inner_both, _, _, out, even, odd, sems = refs

    def fetch(source, start, col_from, width, length, first, col, sem):
        return pltpu.make_async_copy(
            source.at[:, pl.ds(start, length), pl.ds(col_from, width)],
            even.at[:, pl.ds(reach - extra + first, length), pl.ds(col, width)],
            sems.at[sem],
        )

    def part(first, length, block, outer, inner, sem):
        return [
            fetch(block[0], block[1], block[2], cols, length, first, first_col, sem),
            fetch(outer[0], outer[1], outer[2], reach, length, first, outer_col, sem + 1),
            fetch(inner[0], inner[1], inner[2], reach, length, first, inner_col, sem + 2),
        ]

    def move(source, start, col_from, width, length, first, col):
        def one(i, carry):
            for f in range(3):
                even[f, reach - extra + first + i, pl.ds(col, width)] = source[f, start + i, pl.ds(col_from, width)]
            return carry

        lax.fori_loop(0, length, one, 0, unroll=4)

    def moves():
        if stage == MIDDLE:
            size = rows // PIECES
            move(near, 0, 0, cols, rows, rows, first_col)
            move(outer_near, 0, 0, reach, rows, rows, outer_col)
            for i, piece in enumerate(inner_near):
                move(piece, 0, 0, reach, size, rows + i * size, inner_col)
        elif stage == LATE:
            move(far, 0, 0, cols, reach, 2 * rows, first_col)
            slot = reach - extra + 2 * rows
            for side, (col, low_side) in enumerate(((outer_col, is_even), (inner_col, jnp.logical_not(is_even)))):
                for q in range(reach // 2):
                    for f in range(3):
                        packed = far[f, reach + side, pl.ds(q * reach, reach)]
                        even[f, slot + q, pl.ds(col, reach)] = packed
                        even[f, slot + reach - 1 - q, pl.ds(col, reach)] = turned(packed, q, jnp.logical_not(low_side))

    plain, chosen, special = [], [], None
    if stage == EARLY:
        plain = part(0, rows, (own, 0, 0), (outer_both, 0, 0), (inner_both, 0, 0), 0)
    elif stage == MIDDLE:
        chosen = part(rows, rows, (melt, 0, 0), (outer_both, rows, 0), (inner_both, rows, 0), 0)
        special = at_end
    else:
        chosen = part(2 * rows, reach, (melt, 0, 0), (outer_both, rows, 0), (inner_both, rows, 0), 0)
        special = next_end

    def each(act):
        for copy in plain:
            act(copy)
        if special is None:
            return

        @pl.when(special)
        def _():
            for copy in chosen:
                act(copy)

    each(lambda copy: copy.start())
    if stage != LATE:
        token[...] = jnp.zeros_like(token)
    if stage == EARLY:
        for field in range(3):
            for buffer in (even, odd):
                buffer[field, zero_slot] = jnp.zeros_like(buffer[field, zero_slot])
    if stage == LATE:
        half = rows // 2
        first_half = pltpu.make_async_copy(
            even.at[:, pl.ds(2 * reach, half), pl.ds(first_col, cols)], out.at[:, pl.ds(0, half)], sems.at[3]
        )
        first_half.start()
        single = [
            pltpu.make_async_copy(
                even.at[:, pl.ds(2 * reach + p, 1), pl.ds(first_col, cols)], out.at[:, pl.ds(p, 1)], sems.at[8 + p - half]
            )
            for p in range(half, rows)
        ]
        for p, copy in enumerate(single):
            pl.when(p < rows - half - extra)(copy.start)

    if special is not None:
        pl.when(jnp.logical_not(special))(moves)
    each(lambda copy: copy.wait())

    first_missing = reach - extra + rows
    second_missing = reach - extra + 2 * rows

    def substep(k, source, target, cursor, trim):
        next_cursor = cursor + slide_ref[k]
        top = cursor + total_rows - base
        bottom = next_cursor - base
        if stage == EARLY:
            low, high = reach + k + 1, first_missing - 1 - k
        elif stage == MIDDLE:
            low, high = jnp.maximum(first_missing - 1 - k, reach + k + 1), second_missing - 1 - k
        else:
            low, high = second_missing - 1 - k, reach + count - 1 - k

        def advance(group, first, j, carry):
            cut = half_tile if stage == LATE and group <= half_tile else trim
            rows_in = (tiles * TILE - 2 * cut) // TILE
            r = first + group * j if stage == LATE else high - group * (j + 1)
            slots = [r - 1, r] + [jnp.where(r + q < top, r + q, zero_slot) for q in range(1, group + 1)]
            for t in range(rows_in):
                s0 = first_row + cut + TILE * t
                centre = [[source[f, slot, pl.ds(s0, TILE)] for slot in slots] for f in range(3)]
                for i in range(group):
                    slot = slots[1 + i]
                    value, around = [], []
                    for f in range(3):
                        c = centre[f][1 + i]
                        around.append(
                            (centre[f][i] + centre[f][i + 2])
                            + (source[f, slot, pl.ds(s0 - 1, TILE)] + source[f, slot, pl.ds(s0 + 1, TILE)])
                            + (pltpu.roll(c, 1, 1) + pltpu.roll(c, c.shape[1] - 1, 1))
                        )
                        value.append(c)
                    phase, solute, heat = value
                    squared = phase * phase
                    rest = 1.0 - squared
                    drive = (
                        coef_phase * around[0]
                        + phase * ((1.0 - 6.0 * coef_phase + coef_react) - coef_react * squared)
                        - (rest * rest) * (coef_couple * heat + (coef_couple * coef_solute) * solute)
                    )
                    grown = jnp.tanh(drive)
                    change = 0.5 * (grown - phase)
                    result = [
                        grown,
                        (1.0 - 6.0 * coef_diff) * solute + (coef_diff * around[1] + change),
                        (1.0 - 6.0 * coef_heat) * heat + (coef_heat * around[2] + change),
                    ]
                    if t == 0:
                        result = [jnp.where(keep_low[cut], v, 0.0) for v in result]
                    if t == rows_in - 1:
                        result = [jnp.where(keep_high[cut], v, 0.0) for v in result]
                    for f in range(3):
                        target[f, r + i, pl.ds(s0, TILE)] = result[f]
            return carry

        first = low
        for group, following in zip(GROUPS[stage], GROUPS[stage][1:] + GROUPS[stage][-1:]):
            times = jnp.maximum(high - first + following - 1, 0) // group
            lax.fori_loop(0, times, functools.partial(advance, group, first), 0)
            first = first + group * times

        span = pl.ds(first_row, TILE * tiles)

        def clear(r, carry):
            for f in range(3):
                target[f, r, span] = jnp.zeros_like(target[f, r, span])
            return carry

        def keep(r, carry):
            for f in range(3):
                target[f, r, span] = source[f, r, span]
            return carry

        high = jnp.maximum(high, low)

        @pl.when((bottom > low) | (top < high))
        def _():
            lax.fori_loop(low, jnp.clip(bottom, low, high), clear, 0)
            lax.fori_loop(jnp.clip(top, low, high), high, keep, 0)

        return next_cursor

    row = lax.broadcasted_iota(jnp.int32, (TILE, even.shape[3]), 0)
    half_tile = TILE // 2
    keep_low = {0: low_inside, half_tile: low_inside | (row >= half_tile)}
    keep_high = {0: high_inside, half_tile: high_inside | (row < half_tile)}

    def pair(trim):
        def run(j, cursor):
            return substep(2 * j + 1, odd, even, substep(2 * j, even, odd, cursor, trim), trim)

        return run

    wide_pairs = (steps - half_tile) // 2
    cursor = lax.fori_loop(0, wide_pairs, pair(0), jnp.int32(0))
    lax.fori_loop(wide_pairs, steps // 2, pair(half_tile), cursor)

    if stage == LATE:
        for p, copy in enumerate(single):
            pl.when(p >= rows - half - extra)(copy.start)
        first_half.wait()
        for copy in single:
            copy.wait()


def pack_kernel(plan, *refs):
    sources, targets, sems = refs[: plan[0]], refs[plan[0] : -1], refs[-1]
    wide_index = lax.axis_index("wide")
    copies = []
    for i, (source, target, planes, cols, into, side) in enumerate(plan[1]):
        start, width = cols
        if side is not None:
            first, last = (start, width) if side == "inner" else (width, start)
            start = pl.multiple_of(jnp.where(lax.rem(wide_index, 2) == 0, last, first), TILE)
            width = into[3]
        copies.append(
            pltpu.make_async_copy(
                sources[source].at[:, pl.ds(*planes), pl.ds(start, width)],
                targets[target].at[:, pl.ds(into[0], into[1]), pl.ds(into[2], into[3])],
                sems.at[i],
            )
        )
    for copy in copies:
        copy.start()
    for copy in copies:
        copy.wait()


def turned(rows, count, down):
    if count == 0:
        return rows
    return jnp.where(down, pltpu.roll(rows, count, 0), pltpu.roll(rows, rows.shape[0] - count, 0))


def pack_far_kernel(fields, outer, inner, _, block, sem):
    reach, cols = outer.shape[2], fields.shape[2]
    copy = pltpu.make_async_copy(fields.at[:, pl.ds(0, reach)], block.at[:, pl.ds(0, reach)], sem)
    copy.start()
    is_even = lax.rem(lax.axis_index("wide"), 2) == 0
    row = lax.broadcasted_iota(jnp.int32, (reach, fields.shape[3]), 0)
    for side, (strip, low_side) in enumerate(((outer, is_even), (inner, jnp.logical_not(is_even)))):
        for q in range(cols // reach):
            if q >= reach // 2:
                block[:, reach + side, pl.ds(q * reach, reach)] = jnp.zeros((3, reach, fields.shape[3]), jnp.float32)
                continue
            near_rows = (low_side & (row > q)) | (jnp.logical_not(low_side) & (row < reach - 1 - q))
            for f in range(3):
                second = turned(strip[f, reach - 1 - q], q, low_side)
                block[f, reach + side, pl.ds(q * reach, reach)] = jnp.where(near_rows, strip[f, q], second)
    copy.wait()


def pack_far(fields, outer, inner, token):
    reach, (_, _, cols, depth) = outer.shape[2], fields.shape
    operands, specs = place([(fields, pltpu.HBM), (outer, pltpu.VMEM), (inner, pltpu.VMEM), (token, pltpu.VMEM)])
    return pl.pallas_call(
        pack_far_kernel,
        out_shape=pltpu.VMEM((3, reach + 2, cols, depth), jnp.float32),
        in_specs=specs,
        out_specs=pl.BlockSpec(memory_space=pltpu.VMEM),
        scratch_shapes=[pltpu.SemaphoreType.DMA],
        cost_estimate=pl.CostEstimate(flops=0, bytes_accessed=1000, transcendentals=0),
        compiler_params=pltpu.CompilerParams(vmem_limit_bytes=4 * 1024 * 1024),
        name="pack_far",
    )(*operands)


def place(arrays):
    sources, specs = [], []
    for array, space in arrays:
        sources.append(pltpu.with_memory_space_constraint(array, space))
        specs.append(pl.BlockSpec(memory_space=space))
    return sources, specs


def pack(name, sources, shapes, moves, cost=1000):
    sources, specs = place(sources)
    return pl.pallas_call(
        functools.partial(pack_kernel, (len(sources), moves)),
        out_shape=[pltpu.VMEM(shape, jnp.float32) for shape in shapes],
        in_specs=specs,
        out_specs=[pl.BlockSpec(memory_space=pltpu.VMEM)] * len(shapes),
        scratch_shapes=[pltpu.SemaphoreType.DMA((len(moves),))],
        cost_estimate=pl.CostEstimate(flops=0, bytes_accessed=cost, transcendentals=0),
        compiler_params=pltpu.CompilerParams(vmem_limit_bytes=4 * 1024 * 1024),
        name=name,
    )(*sources)


def run_stage(stage, shape, slide_rows, arrays, state=()):
    _, rows, cols, depth = shape
    reach = slide_rows.shape[0]
    anywhere = pl.BlockSpec(memory_space=pl.ANY)
    in_vmem = pl.BlockSpec(memory_space=pltpu.VMEM)
    held = pltpu.VMEM((3, rows + 4 * reach + 1, cols + 4 * TILE, depth), jnp.float32)
    operands, in_specs = place([(slide_rows, pltpu.VMEM)] + arrays + [(s, pltpu.VMEM) for s in state])
    out_shape, out_specs = [held, held], [in_vmem, in_vmem]
    if stage != LATE:
        out_shape, out_specs = [held, held, pltpu.VMEM((TILE, depth), jnp.float32)], [in_vmem] * 3
    if stage == LATE:
        out_shape, out_specs = [jax.ShapeDtypeStruct(shape, jnp.float32)] + out_shape, [anywhere] + out_specs
    offset = 1 if stage == LATE else 0
    aliases = {len(operands) - 2 + i: offset + i for i in range(2)} if state else {}
    return pl.pallas_call(
        functools.partial(stage_kernel, stage, rows, cols),
        out_shape=out_shape,
        in_specs=in_specs,
        out_specs=out_specs,
        input_output_aliases=aliases,
        scratch_shapes=[pltpu.SemaphoreType.DMA((8 + max(PIECES, rows // 2),)), pltpu.SMEM((reach,), jnp.int32)],
        cost_estimate=pl.CostEstimate(flops=MIDDLE_FLOPS if stage == MIDDLE else 0, bytes_accessed=1000, transcendentals=0),
        compiler_params=pltpu.CompilerParams(vmem_limit_bytes=16 * 1024 * 1024),
        name=("early", "middle", "late")[stage],
    )(*operands)


def body(fields, melt_planes, slide_planes):
    rows, cols, depth = fields.shape[1:]
    reach = slide_planes.shape[0]
    split = rows // 2
    wide = lax.axis_size("wide")
    inner_pairs = [(a, a + 1) for a in range(0, wide - 1, 2)]
    outer_pairs = [(a, a + 1) for a in range(1, wide - 1, 2)]
    is_even = lax.rem(lax.axis_index("wide"), 2) == 0
    inner_start = jnp.where(is_even, cols - reach, 0)

    def edge(block):
        return lax.dynamic_slice_in_dim(block, inner_start, reach, 2)

    def far_away(array):
        return (array, pltpu.HBM)

    def close(array):
        return (array, pltpu.VMEM)

    ends = (0, cols - reach)
    near = passed(fields, -1)
    outer_own, outer_pair, inner_pair = pack(
        "pack_strips",
        [far_away(fields), far_away(melt_planes)],
        [(3, rows, reach, depth), (3, 2 * rows, reach, depth), (3, 2 * rows, reach, depth)],
        [
            (0, 0, (0, rows), ends, (0, rows, 0, reach), "outer"),
            (0, 1, (0, rows), ends, (0, rows, 0, reach), "outer"),
            (1, 1, (0, rows), ends, (rows, rows, 0, reach), "outer"),
            (0, 2, (0, rows), ends, (0, rows, 0, reach), "inner"),
            (1, 2, (0, rows), ends, (rows, rows, 0, reach), "inner"),
        ],
    )
    outer_near = passed(outer_own, -1, outer_pairs)
    outer_both = passed(outer_pair, 0, outer_pairs)
    inner_both = passed(inner_pair, 0, inner_pairs)
    slide_rows = jnp.broadcast_to(slide_planes[:, None], (reach, depth))
    run = functools.partial(run_stage, shape=fields.shape, slide_rows=slide_rows)
    both = [close(outer_both), close(inner_both)]
    *state, token = run(EARLY, arrays=[far_away(fields), *both])
    far_block = pack_far(fields, outer_both, inner_both, token)
    far = passed(far_block, -2)
    size = rows // PIECES
    edges = pack(
        "pack_edge",
        [close(near), close(token)],
        [(3, size, reach, depth)] * PIECES,
        [(0, i, (i * size, size), ends, (0, size, 0, reach), "inner") for i in range(PIECES)],
    )
    inner_near = [close(passed(piece, 0, inner_pairs)) for piece in edges]
    *state, _ = run(
        MIDDLE, arrays=[close(near), far_away(melt_planes), *both, close(outer_near), *inner_near], state=state
    )
    return run(LATE, arrays=[close(far), far_away(melt_planes), *both], state=state)[0]


def solution(mesh):
    return jax.shard_map(
        body,
        mesh=mesh,
        in_specs=(P(None, "grow", "wide", None), P(None, None, "wide", None), P()),
        out_specs=P(None, "grow", "wide", None),
        check_vma=False,
    )
```

profile of v0, /device:TPU:1, one launch (start us, length us, event | category | flops | bytes accessed | tf_op | source)
XLA Modules:
  0.0 38.1 jit_solution(15342607414987307674)
XLA Ops:
  0.0 1.3 %collective-permute-start.3 = (f32[3,16,32,128]{3,2,1,0:T(8,128)}, f32[3,16,32,128]{3,2,1,0:T(8,128)S(1)}, u32[]{:S(2)}, u32[]{:S(2)}) collective-permute-start(f32[3,16,32,128]{3,2,1,0:T(8,128)} %fields.1), channel_id=1, source_target_pairs={{4,0},{8,4},{12,8},{16,12},{20,16},{24,20},{28,24},{5,1},{9,5},{13... | collective-permute-start | bytes 2359304 | tf_op jit(solution)/shard_map/ppermute | solution.py:27
  1.3 1.4 %pack_strips.1 = (f32[3,16,8,128]{3,2,1,0:T(8,128)S(1)}, f32[3,32,8,128]{3,2,1,0:T(8,128)S(1)}, f32[3,32,8,128]{3,2,1,0:T(8,128)S(1)}) custom-call(f32[3,16,32,128]{3,2,1,0:T(8,128)} %fields.1, f32[3,16,32,128]{3,2,1,0:T(8,128)} %refs_1_.5), custom_call_target="tpu_custom_call" | custom-call | bytes 1000 | tf_op jit(solution)/shard_map/pack_strips/pallas_call | solution.py:340
  2.7 4.5 %collective-permute-start = (f32[3,32,8,128]{3,2,1,0:T(8,128)S(1)}, f32[3,32,8,128]{3,2,1,0:T(8,128)S(1)}, u32[]{:S(2)}, u32[]{:S(2)}) collective-permute-start(f32[3,32,8,128]{3,2,1,0:T(8,128)S(1)} %get-tuple-element.16), channel_id=1, source_target_pairs={{1,2},{2,1},{5,6},{6,5},{9,10},{10,9},{13,14},{14,13},{17,18},{18,... | collective-permute-start | bytes 1179656 | tf_op jit(solution)/shard_map/ppermute | solution.py:30
  7.2 0.1 collective-permute-start.1
  7.3 1.3 %collective-permute-start.4 = (f32[3,16,8,128]{3,2,1,0:T(8,128)S(1)}, f32[3,16,8,128]{3,2,1,0:T(8,128)S(1)}, u32[]{:S(2)}, u32[]{:S(2)}) collective-permute-start(f32[3,16,8,128]{3,2,1,0:T(8,128)S(1)} %get-tuple-element.19), channel_id=1, source_target_pairs={{5,2},{6,1},{9,6},{10,5},{13,10},{14,9},{17,14},{18,13},{21,18},{2... | collective-permute-start | bytes 589832 | tf_op jit(solution)/shard_map/ppermute | solution.py:37
  8.6 4.4 %collective-permute-done.refs_1_.outer.refs_2_ = f32[3,32,8,128]{3,2,1,0:T(8,128)S(1)} collective-permute-done((f32[3,32,8,128]{3,2,1,0:T(8,128)S(1)}, f32[3,32,8,128]{3,2,1,0:T(8,128)S(1)}, u32[]{:S(2)}, u32[]{:S(2)}) %collective-permute-start) | collective-permute-done | bytes 393248 | tf_op jit(solution)/shard_map/ppermute | solution.py:30
  12.9 0.0 collective-permute-done.1.refs_2_.inner.refs_3_
  12.9 0.7 %broadcast_in_dim.2.slide_rows = s32[8,128]{1,0:T(8,128)S(1)} broadcast(s32[8]{0:T(128)} %param.5), dimensions={0} | broadcast | bytes 4128 | tf_op jit(solution)/shard_map/broadcast_in_dim | solution.py:415
  13.7 5.0 %early.1 = (f32[3,49,64,128]{3,2,1,0:T(8,128)S(1)}, f32[3,49,64,128]{3,2,1,0:T(8,128)S(1)}, f32[8,128]{1,0:T(8,128)S(1)}) custom-call(s32[8,128]{1,0:T(8,128)S(1)} %broadcast_in_dim.2.slide_rows, f32[3,16,32,128]{3,2,1,0:T(8,128)} %fields.1, f32[3,32,8,128]{3,2,1,0:T(8,128)S(1)} %collective-permute-done.refs_1_.outer.refs_2_, ...), custom_call_target="tpu_custom_call" | custom-call | bytes 1000 | tf_op jit(solution)/shard_map/early/pallas_call | solution.py:366
  18.7 1.0 %pack_far.1 = f32[3,10,32,128]{3,2,1,0:T(8,128)S(1)} custom-call(f32[3,16,32,128]{3,2,1,0:T(8,128)} %fields.1, f32[3,32,8,128]{3,2,1,0:T(8,128)S(1)} %collective-permute-done.refs_1_.outer.refs_2_, f32[3,32,8,128]{3,2,1,0:T(8,128)S(1)} %collective-permute-done.1.refs_2_.inner.refs_3_, f32[8,128]{1,0:T(8,128)S(1)} %get-tuple-element.18._.refs_1_), custom_call_target="tpu_custom_call" | custom-call | bytes 1000 | tf_op jit(solution)/shard_map/pack_far/pallas_call | solution.py:318
  19.7 1.3 %collective-permute-start.2 = (f32[3,10,32,128]{3,2,1,0:T(8,128)S(1)}, f32[3,10,32,128]{3,2,1,0:T(8,128)S(1)}, u32[]{:S(2)}, u32[]{:S(2)}) collective-permute-start(f32[3,10,32,128]{3,2,1,0:T(8,128)S(1)} %pack_far.1), channel_id=1, source_target_pairs={{8,0},{12,4},{16,8},{20,12},{24,16},{28,20},{9,1},{13,5},{17,9},{2... | collective-permute-start | bytes 1474568 | tf_op jit(solution)/shard_map/ppermute | solution.py:27
  21.0 0.4 %collective-permute-done.3.refs_0_ = f32[3,16,32,128]{3,2,1,0:T(8,128)S(1)} collective-permute-done((f32[3,16,32,128]{3,2,1,0:T(8,128)}, f32[3,16,32,128]{3,2,1,0:T(8,128)S(1)}, u32[]{:S(2)}, u32[]{:S(2)}) %collective-permute-start.3) | collective-permute-done | bytes 786464 | tf_op jit(solution)/shard_map/ppermute | solution.py:27
  21.5 2.1 %collective-permute-start.5 = (f32[3,8,8,128]{3,2,1,0:T(8,128)S(1)}, f32[3,8,8,128]{3,2,1,0:T(8,128)S(1)}, u32[]{:S(2)}, u32[]{:S(2)}) collective-permute-start(f32[3,8,8,128]{3,2,1,0:T(8,128)S(1)} %get-tuple-element.20), channel_id=1, source_target_pairs={{0,1},{2,3},{1,0},{3,2},{4,5},{6,7},{5,4},{7,6},{8,9},{10,11},{9,8... | collective-permute-start | bytes 294920 | tf_op jit(solution)/shard_map/ppermute | solution.py:30
  23.6 0.1 collective-permute-start.6
  23.7 1.6 %collective-permute-done.4.refs_4_ = f32[3,16,8,128]{3,2,1,0:T(8,128)S(1)} collective-permute-done((f32[3,16,8,128]{3,2,1,0:T(8,128)S(1)}, f32[3,16,8,128]{3,2,1,0:T(8,128)S(1)}, u32[]{:S(2)}, u32[]{:S(2)}) %collective-permute-start.4) | collective-permute-done | bytes 196640 | tf_op jit(solution)/shard_map/ppermute | solution.py:37
  25.3 0.0 collective-permute-done.5.refs_5_
  25.3 0.0 collective-permute-done.6.refs_6_
  25.3 6.3 %middle.1 = (f32[3,49,64,128]{3,2,1,0:T(8,128)S(1)}, f32[3,49,64,128]{3,2,1,0:T(8,128)S(1)}, f32[8,128]{1,0:T(8,128)}) custom-call(s32[8,128]{1,0:T(8,128)S(1)} %broadcast_in_dim.2.slide_rows, f32[3,16,32,128]{3,2,1,0:T(8,128)S(1)} %collective-permute-done.3.refs_0_, f32[3,16,32,128]{3,2,1,0:T(8,128)} %refs_1_.5, ...), custom_call_target="tpu_custom_call", output_to_operand_aliasing={{0}: (8, {}), {1}: (9, {})} | custom-call | flops 3500000000 | bytes 1000 | tf_op jit(solution)/shard_map/middle/pallas_call | solution.py:366
  31.5 4.2 %collective-permute-done.2.refs_0_ = f32[3,10,32,128]{3,2,1,0:T(8,128)S(1)} collective-permute-done((f32[3,10,32,128]{3,2,1,0:T(8,128)S(1)}, f32[3,10,32,128]{3,2,1,0:T(8,128)S(1)}, u32[]{:S(2)}, u32[]{:S(2)}) %collective-permute-start.2) | collective-permute-done | bytes 491552 | tf_op jit(solution)/shard_map/ppermute | solution.py:27
  35.8 2.3 %late.1 = (f32[3,16,32,128]{3,2,1,0:T(8,128)}, f32[3,49,64,128]{3,2,1,0:T(8,128)S(1)}, f32[3,49,64,128]{3,2,1,0:T(8,128)S(1)}) custom-call(s32[8,128]{1,0:T(8,128)S(1)} %broadcast_in_dim.2.slide_rows, f32[3,10,32,128]{3,2,1,0:T(8,128)S(1)} %collective-permute-done.2.refs_0_, ...), custom_call_target="tpu_custom_call", output_to_operand_aliasing={{1}: (5, {}), {2}: (6, {})} | custom-call | bytes 1000 | tf_op jit(solution)/shard_map/late/pallas_call | solution.py:366
  (1 shorter events, 0.0 us)
Async XLA Ops:
  0.0 21.4 %collective-permute-start.3 = (f32[3,16,32,128]{3,2,1,0:T(8,128)}, f32[3,16,32,128]{3,2,1,0:T(8,128)S(1)}, u32[]{:S(2)}, u32[]{:S(2)}) collective-permute-start(f32[3,16,32,128]{3,2,1,0:T(8,128)} %fields.1), channel_id=1, source_target_pairs={{4,0},{8,4},{12,8},{16,12},{20,16},{24,20},{28,24},{5,1},{9,5},{13... | collective-permute-start | bytes 2359304 | tf_op jit(solution)/shard_map/ppermute | solution.py:27
  2.7 10.3 %collective-permute-start = (f32[3,32,8,128]{3,2,1,0:T(8,128)S(1)}, f32[3,32,8,128]{3,2,1,0:T(8,128)S(1)}, u32[]{:S(2)}, u32[]{:S(2)}) collective-permute-start(f32[3,32,8,128]{3,2,1,0:T(8,128)S(1)} %get-tuple-element.16), channel_id=1, source_target_pairs={{1,2},{2,1},{5,6},{6,5},{9,10},{10,9},{13,14},{14,13},{17,18},{18,... | collective-permute-start | bytes 1179656 | tf_op jit(solution)/shard_map/ppermute | solution.py:30
  7.2 5.7 %collective-permute-start.1 = (f32[3,32,8,128]{3,2,1,0:T(8,128)S(1)}, f32[3,32,8,128]{3,2,1,0:T(8,128)S(1)}, u32[]{:S(2)}, u32[]{:S(2)}) collective-permute-start(f32[3,32,8,128]{3,2,1,0:T(8,128)S(1)} %get-tuple-element.17), channel_id=1, source_target_pairs={{0,1},{2,3},{1,0},{3,2},{4,5},{6,7},{5,4},{7,6},{8,9},{10,11},{9,8... | collective-permute-start | bytes 1179656 | tf_op jit(solution)/shard_map/ppermute | solution.py:30
  7.3 18.0 %collective-permute-start.4 = (f32[3,16,8,128]{3,2,1,0:T(8,128)S(1)}, f32[3,16,8,128]{3,2,1,0:T(8,128)S(1)}, u32[]{:S(2)}, u32[]{:S(2)}) collective-permute-start(f32[3,16,8,128]{3,2,1,0:T(8,128)S(1)} %get-tuple-element.19), channel_id=1, source_target_pairs={{5,2},{6,1},{9,6},{10,5},{13,10},{14,9},{17,14},{18,13},{21,18},{2... | collective-permute-start | bytes 589832 | tf_op jit(solution)/shard_map/ppermute | solution.py:37
  19.7 16.1 %collective-permute-start.2 = (f32[3,10,32,128]{3,2,1,0:T(8,128)S(1)}, f32[3,10,32,128]{3,2,1,0:T(8,128)S(1)}, u32[]{:S(2)}, u32[]{:S(2)}) collective-permute-start(f32[3,10,32,128]{3,2,1,0:T(8,128)S(1)} %pack_far.1), channel_id=1, source_target_pairs={{8,0},{12,4},{16,8},{20,12},{24,16},{28,20},{9,1},{13,5},{17,9},{2... | collective-permute-start | bytes 1474568 | tf_op jit(solution)/shard_map/ppermute | solution.py:27
  21.5 3.8 %collective-permute-start.5 = (f32[3,8,8,128]{3,2,1,0:T(8,128)S(1)}, f32[3,8,8,128]{3,2,1,0:T(8,128)S(1)}, u32[]{:S(2)}, u32[]{:S(2)}) collective-permute-start(f32[3,8,8,128]{3,2,1,0:T(8,128)S(1)} %get-tuple-element.20), channel_id=1, source_target_pairs={{0,1},{2,3},{1,0},{3,2},{4,5},{6,7},{5,4},{7,6},{8,9},{10,11},{9,8... | collective-permute-start | bytes 294920 | tf_op jit(solution)/shard_map/ppermute | solution.py:30
  23.6 1.7 %collective-permute-start.6 = (f32[3,8,8,128]{3,2,1,0:T(8,128)S(1)}, f32[3,8,8,128]{3,2,1,0:T(8,128)S(1)}, u32[]{:S(2)}, u32[]{:S(2)}) collective-permute-start(f32[3,8,8,128]{3,2,1,0:T(8,128)S(1)} %get-tuple-element.21), channel_id=1, source_target_pairs={{0,1},{2,3},{1,0},{3,2},{4,5},{6,7},{5,4},{7,6},{8,9},{10,11},{9,8... | collective-permute-start | bytes 294920 | tf_op jit(solution)/shard_map/ppermute | solution.py:30
where the time goes:
time: 38.7 us; the launch traced here: 38.1 us
  Pallas kernels  16 us (41%)
  starting transfers between devices  10.7 us (28%)
  waiting for transfers between devices  10.6 us (27%)
  local copies, waits for them, and re-layouts  0.72 us (2%)
    pallas_call x3, Pallas kernels, run_stage(): pl.pallas_call(functools.partial(stage_kernel, stage, rows, cols), out_sh...  13.6 us
    ppermute x4, starting transfers between devices, passed(): return lax.ppermute(value, 'wide', lanes)  6.81 us
    ppermute x2, waiting for transfers between devices, passed(): lax.ppermute(value, 'grow', [(g, g + grow_step) for g in range(grow) if 0...  4.65 us
    ppermute x4, waiting for transfers between devices, passed(): return lax.ppermute(value, 'wide', lanes)  4.37 us
    ppermute x2, starting transfers between devices, passed(): lax.ppermute(value, 'grow', [(g, g + grow_step) for g in range(grow) if 0...  2.57 us
    ppermute x1, waiting for transfers between devices, passed(): return lax.ppermute(value, ('grow', 'wide'), pairs)  1.59 us
    pallas_call x2, Pallas kernels, pack(): pl.pallas_call(functools.partial(pack_kernel, (len(sources), moves)), out...  1.41 us
    ppermute x1, starting transfers between devices, passed(): return lax.ppermute(value, ('grow', 'wide'), pairs)  1.29 us
  transfers between devices with their start and end apart: 7, of which 4 were waited for; matrix products, arithmetic and copies ran while one was open for 2% of the time, Pallas kernels for 36%

commit v1 on v0

--- a/solution.py
+++ b/solution.py
@@ -9,7 +9,8 @@
 
 TILE = 8
 EARLY, MIDDLE, LATE = 0, 1, 2
-GROUPS = ((6,), (16,), (8, 4, 2))
+EARLY_GROUP = 6
+LATE_GROUPS = (8, 6, 4, 2)
 PIECES = 2
 MIDDLE_FLOPS = 3_500_000_000
 
@@ -162,7 +163,7 @@
     first_missing = reach - extra + rows
     second_missing = reach - extra + 2 * rows
 
-    def substep(k, source, target, cursor, trim):
+    def substep(k, source, target, cursor, trim, group):
         next_cursor = cursor + slide_ref[k]
         top = cursor + total_rows - base
         bottom = next_cursor - base
@@ -173,10 +174,10 @@
         else:
             low, high = second_missing - 1 - k, reach + count - 1 - k
 
-        def advance(group, first, j, carry):
+        def advance(j, carry):
             cut = half_tile if stage == LATE and group <= half_tile else trim
             rows_in = (tiles * TILE - 2 * cut) // TILE
-            r = first + group * j if stage == LATE else high - group * (j + 1)
+            r = low if stage == LATE else high - group * (j + 1)
             slots = [r - 1, r] + [jnp.where(r + q < top, r + q, zero_slot) for q in range(1, group + 1)]
             for t in range(rows_in):
                 s0 = first_row + cut + TILE * t
@@ -207,19 +208,18 @@
                         (1.0 - 6.0 * coef_diff) * solute + (coef_diff * around[1] + change),
                         (1.0 - 6.0 * coef_heat) * heat + (coef_heat * around[2] + change),
                     ]
-                    if t == 0:
+                    if t == 0 and cut < TILE:
                         result = [jnp.where(keep_low[cut], v, 0.0) for v in result]
-                    if t == rows_in - 1:
+                    if t == rows_in - 1 and cut < TILE:
                         result = [jnp.where(keep_high[cut], v, 0.0) for v in result]
                     for f in range(3):
                         target[f, r + i, pl.ds(s0, TILE)] = result[f]
             return carry
 
-        first = low
-        for group, following in zip(GROUPS[stage], GROUPS[stage][1:] + GROUPS[stage][-1:]):
-            times = jnp.maximum(high - first + following - 1, 0) // group
-            lax.fori_loop(0, times, functools.partial(advance, group, first), 0)
-            first = first + group * times
+        if stage == EARLY:
+            lax.fori_loop(0, jnp.maximum(high - low + group - 1, 0) // group, advance, 0)
+        else:
+            advance(0, 0)
 
         span = pl.ds(first_row, TILE * tiles)
 
@@ -244,18 +244,30 @@
 
     row = lax.broadcasted_iota(jnp.int32, (TILE, even.shape[3]), 0)
     half_tile = TILE // 2
-    keep_low = {0: low_inside, half_tile: low_inside | (row >= half_tile)}
-    keep_high = {0: high_inside, half_tile: high_inside | (row < half_tile)}
-
-    def pair(trim):
-        def run(j, cursor):
-            return substep(2 * j + 1, odd, even, substep(2 * j, even, odd, cursor, trim), trim)
-
-        return run
-
-    wide_pairs = (steps - half_tile) // 2
-    cursor = lax.fori_loop(0, wide_pairs, pair(0), jnp.int32(0))
-    lax.fori_loop(wide_pairs, steps // 2, pair(half_tile), cursor)
+    keep_low = {0: low_inside, half_tile: low_inside | (row >= half_tile), TILE: True}
+    keep_high = {0: high_inside, half_tile: high_inside | (row < half_tile), TILE: True}
+
+    def advance_all(group):
+        def pair(trim):
+            def run(j, cursor):
+                return substep(2 * j + 1, odd, even, substep(2 * j, even, odd, cursor, trim, group), trim, group)
+
+            return run
+
+        wide_pairs = (steps - half_tile) // 2
+        cursor = lax.fori_loop(0, wide_pairs, pair(0), jnp.int32(0))
+        lax.fori_loop(wide_pairs, steps // 2, pair(half_tile), cursor)
+
+    if stage == EARLY:
+        advance_all(EARLY_GROUP)
+    elif stage == MIDDLE:
+        cursor = jnp.int32(0)
+        for k in range(steps):
+            buffers = (even, odd) if k % 2 == 0 else (odd, even)
+            cursor = substep(k, *buffers, cursor, (k + 1) // half_tile * half_tile, rows)
+    else:
+        for group, smaller in zip(LATE_GROUPS, LATE_GROUPS[1:] + (0,)):
+            pl.when((extra > smaller) & (extra <= group))(functools.partial(advance_all, group))
 
     if stage == LATE:
         for p, copy in enumerate(single):

time: 38.7 us -> 39.7 us (1.026)
  waiting for transfers between devices: 10.6 us -> 13 us
  Pallas kernels: 16 us -> 14.6 us
    ppermute x2, waiting for transfers between devices: 4.65 us -> 7.03 us  [passed(): lax.ppermute(value, 'grow', [(g, g + grow_step) for g in range(grow) if 0...]
    pallas_call x3, Pallas kernels: 13.6 us -> 12.1 us  [run_stage(): pl.pallas_call(functools.partial(stage_kernel, stage, rows, cols), out_sh...]
  transfers between devices with their start and end apart: 7 -> 7, of which waited for: 4 -> 4; matrix products, arithmetic and copies ran while one was open for 2% -> 2% of each run, Pallas kernels for 36% -> 29%
where the time goes in v1:
time: 39.7 us; the launch traced here: 39 us
  Pallas kernels  14.6 us (37%)
  waiting for transfers between devices  13 us (33%)
  starting transfers between devices  10.7 us (27%)
  local copies, waits for them, and re-layouts  0.72 us (2%)
    pallas_call x3, Pallas kernels, run_stage(): pl.pallas_call(functools.partial(stage_kernel, stage, rows, cols), out_sh...  12.1 us
    ppermute x2, waiting for transfers between devices, passed(): lax.ppermute(value, 'grow', [(g, g + grow_step) for g in range(grow) if 0...  7.03 us
    ppermute x4, starting transfers between devices, passed(): return lax.ppermute(value, 'wide', lanes)  6.81 us
    ppermute x4, waiting for transfers between devices, passed(): return lax.ppermute(value, 'wide', lanes)  4.37 us
    ppermute x2, starting transfers between devices, passed(): lax.ppermute(value, 'grow', [(g, g + grow_step) for g in range(grow) if 0...  2.57 us
    ppermute x1, waiting for transfers between devices, passed(): return lax.ppermute(value, ('grow', 'wide'), pairs)  1.59 us
    pallas_call x2, Pallas kernels, pack(): pl.pallas_call(functools.partial(pack_kernel, (len(sources), moves)), out...  1.41 us
    ppermute x1, starting transfers between devices, passed(): return lax.ppermute(value, ('grow', 'wide'), pairs)  1.29 us
  transfers between devices with their start and end apart: 7, of which 4 were waited for; matrix products, arithmetic and copies ran while one was open for 2% of the time, Pallas kernels for 29%

profile of v1, /device:TPU:1, one launch (start us, length us, event | category | flops | bytes accessed | tf_op | source)
XLA Modules:
  0.0 39.0 jit_solution(9315975053234362795)
XLA Ops:
  0.0 1.3 %collective-permute-start.3 = (f32[3,16,32,128]{3,2,1,0:T(8,128)}, f32[3,16,32,128]{3,2,1,0:T(8,128)S(1)}, u32[]{:S(2)}, u32[]{:S(2)}) collective-permute-start(f32[3,16,32,128]{3,2,1,0:T(8,128)} %fields.1), channel_id=1, source_target_pairs={{4,0},{8,4},{12,8},{16,12},{20,16},{24,20},{28,24},{5,1},{9,5},{13... | collective-permute-start | bytes 2359304 | tf_op jit(solution)/shard_map/ppermute | solution.py:28
  1.3 1.4 %pack_strips.1 = (f32[3,16,8,128]{3,2,1,0:T(8,128)S(1)}, f32[3,32,8,128]{3,2,1,0:T(8,128)S(1)}, f32[3,32,8,128]{3,2,1,0:T(8,128)S(1)}) custom-call(f32[3,16,32,128]{3,2,1,0:T(8,128)} %fields.1, f32[3,16,32,128]{3,2,1,0:T(8,128)} %refs_1_.5), custom_call_target="tpu_custom_call" | custom-call | bytes 1000 | tf_op jit(solution)/shard_map/pack_strips/pallas_call | solution.py:352
  2.7 4.5 %collective-permute-start = (f32[3,32,8,128]{3,2,1,0:T(8,128)S(1)}, f32[3,32,8,128]{3,2,1,0:T(8,128)S(1)}, u32[]{:S(2)}, u32[]{:S(2)}) collective-permute-start(f32[3,32,8,128]{3,2,1,0:T(8,128)S(1)} %get-tuple-element.16), channel_id=1, source_target_pairs={{1,2},{2,1},{5,6},{6,5},{9,10},{10,9},{13,14},{14,13},{17,18},{18,... | collective-permute-start | bytes 1179656 | tf_op jit(solution)/shard_map/ppermute | solution.py:31
  7.2 0.1 collective-permute-start.1
  7.3 1.3 %collective-permute-start.4 = (f32[3,16,8,128]{3,2,1,0:T(8,128)S(1)}, f32[3,16,8,128]{3,2,1,0:T(8,128)S(1)}, u32[]{:S(2)}, u32[]{:S(2)}) collective-permute-start(f32[3,16,8,128]{3,2,1,0:T(8,128)S(1)} %get-tuple-element.19), channel_id=1, source_target_pairs={{5,2},{6,1},{9,6},{10,5},{13,10},{14,9},{17,14},{18,13},{21,18},{2... | collective-permute-start | bytes 589832 | tf_op jit(solution)/shard_map/ppermute | solution.py:38
  8.6 4.4 %collective-permute-done.refs_1_.outer.refs_2_ = f32[3,32,8,128]{3,2,1,0:T(8,128)S(1)} collective-permute-done((f32[3,32,8,128]{3,2,1,0:T(8,128)S(1)}, f32[3,32,8,128]{3,2,1,0:T(8,128)S(1)}, u32[]{:S(2)}, u32[]{:S(2)}) %collective-permute-start) | collective-permute-done | bytes 393248 | tf_op jit(solution)/shard_map/ppermute | solution.py:31
  12.9 0.0 collective-permute-done.1.refs_2_.inner.refs_3_
  12.9 0.7 %broadcast_in_dim.2.slide_rows = s32[8,128]{1,0:T(8,128)S(1)} broadcast(s32[8]{0:T(128)} %param.5), dimensions={0} | broadcast | bytes 4128 | tf_op jit(solution)/shard_map/broadcast_in_dim | solution.py:427
  13.7 3.0 %early.1 = (f32[3,49,64,128]{3,2,1,0:T(8,128)S(1)}, f32[3,49,64,128]{3,2,1,0:T(8,128)S(1)}, f32[8,128]{1,0:T(8,128)S(1)}) custom-call(s32[8,128]{1,0:T(8,128)S(1)} %broadcast_in_dim.2.slide_rows, f32[3,16,32,128]{3,2,1,0:T(8,128)} %fields.1, f32[3,32,8,128]{3,2,1,0:T(8,128)S(1)} %collective-permute-done.refs_1_.outer.refs_2_, ...), custom_call_target="tpu_custom_call" | custom-call | bytes 1000 | tf_op jit(solution)/shard_map/early/pallas_call | solution.py:378
  16.7 1.0 %pack_far.1 = f32[3,10,32,128]{3,2,1,0:T(8,128)S(1)} custom-call(f32[3,16,32,128]{3,2,1,0:T(8,128)} %fields.1, f32[3,32,8,128]{3,2,1,0:T(8,128)S(1)} %collective-permute-done.refs_1_.outer.refs_2_, f32[3,32,8,128]{3,2,1,0:T(8,128)S(1)} %collective-permute-done.1.refs_2_.inner.refs_3_, f32[8,128]{1,0:T(8,128)S(1)} %get-tuple-element.18._.refs_1_), custom_call_target="tpu_custom_call" | custom-call | bytes 1000 | tf_op jit(solution)/shard_map/pack_far/pallas_call | solution.py:330
  17.7 1.3 %collective-permute-start.2 = (f32[3,10,32,128]{3,2,1,0:T(8,128)S(1)}, f32[3,10,32,128]{3,2,1,0:T(8,128)S(1)}, u32[]{:S(2)}, u32[]{:S(2)}) collective-permute-start(f32[3,10,32,128]{3,2,1,0:T(8,128)S(1)} %pack_far.1), channel_id=1, source_target_pairs={{8,0},{12,4},{16,8},{20,12},{24,16},{28,20},{9,1},{13,5},{17,9},{2... | collective-permute-start | bytes 1474568 | tf_op jit(solution)/shard_map/ppermute | solution.py:28
  19.0 2.4 %collective-permute-done.3.refs_0_ = f32[3,16,32,128]{3,2,1,0:T(8,128)S(1)} collective-permute-done((f32[3,16,32,128]{3,2,1,0:T(8,128)}, f32[3,16,32,128]{3,2,1,0:T(8,128)S(1)}, u32[]{:S(2)}, u32[]{:S(2)}) %collective-permute-start.3) | collective-permute-done | bytes 786464 | tf_op jit(solution)/shard_map/ppermute | solution.py:28
  21.5 2.1 %collective-permute-start.5 = (f32[3,8,8,128]{3,2,1,0:T(8,128)S(1)}, f32[3,8,8,128]{3,2,1,0:T(8,128)S(1)}, u32[]{:S(2)}, u32[]{:S(2)}) collective-permute-start(f32[3,8,8,128]{3,2,1,0:T(8,128)S(1)} %get-tuple-element.20), channel_id=1, source_target_pairs={{0,1},{2,3},{1,0},{3,2},{4,5},{6,7},{5,4},{7,6},{8,9},{10,11},{9,8... | collective-permute-start | bytes 294920 | tf_op jit(solution)/shard_map/ppermute | solution.py:31
  23.6 0.1 collective-permute-start.6
  23.7 1.6 %collective-permute-done.4.refs_4_ = f32[3,16,8,128]{3,2,1,0:T(8,128)S(1)} collective-permute-done((f32[3,16,8,128]{3,2,1,0:T(8,128)S(1)}, f32[3,16,8,128]{3,2,1,0:T(8,128)S(1)}, u32[]{:S(2)}, u32[]{:S(2)}) %collective-permute-start.4) | collective-permute-done | bytes 196640 | tf_op jit(solution)/shard_map/ppermute | solution.py:38
  25.3 0.0 collective-permute-done.5.refs_5_
  25.3 0.0 collective-permute-done.6.refs_6_
  25.3 5.9 %middle.1 = (f32[3,49,64,128]{3,2,1,0:T(8,128)S(1)}, f32[3,49,64,128]{3,2,1,0:T(8,128)S(1)}, f32[8,128]{1,0:T(8,128)}) custom-call(s32[8,128]{1,0:T(8,128)S(1)} %broadcast_in_dim.2.slide_rows, f32[3,16,32,128]{3,2,1,0:T(8,128)S(1)} %collective-permute-done.3.refs_0_, f32[3,16,32,128]{3,2,1,0:T(8,128)} %refs_1_.5, ...), custom_call_target="tpu_custom_call", output_to_operand_aliasing={{0}: (8, {}), {1}: (9, {})} | custom-call | flops 3500000000 | bytes 1000 | tf_op jit(solution)/shard_map/middle/pallas_call | solution.py:378
  31.1 4.6 %collective-permute-done.2.refs_0_ = f32[3,10,32,128]{3,2,1,0:T(8,128)S(1)} collective-permute-done((f32[3,10,32,128]{3,2,1,0:T(8,128)S(1)}, f32[3,10,32,128]{3,2,1,0:T(8,128)S(1)}, u32[]{:S(2)}, u32[]{:S(2)}) %collective-permute-start.2) | collective-permute-done | bytes 491552 | tf_op jit(solution)/shard_map/ppermute | solution.py:28
  35.8 3.3 %late.1 = (f32[3,16,32,128]{3,2,1,0:T(8,128)}, f32[3,49,64,128]{3,2,1,0:T(8,128)S(1)}, f32[3,49,64,128]{3,2,1,0:T(8,128)S(1)}) custom-call(s32[8,128]{1,0:T(8,128)S(1)} %broadcast_in_dim.2.slide_rows, f32[3,10,32,128]{3,2,1,0:T(8,128)S(1)} %collective-permute-done.2.refs_0_, ...), custom_call_target="tpu_custom_call", output_to_operand_aliasing={{1}: (5, {}), {2}: (6, {})} | custom-call | bytes 1000 | tf_op jit(solution)/shard_map/late/pallas_call | solution.py:378
  (1 shorter events, 0.0 us)
Async XLA Ops:
  0.0 21.4 %collective-permute-start.3 = (f32[3,16,32,128]{3,2,1,0:T(8,128)}, f32[3,16,32,128]{3,2,1,0:T(8,128)S(1)}, u32[]{:S(2)}, u32[]{:S(2)}) collective-permute-start(f32[3,16,32,128]{3,2,1,0:T(8,128)} %fields.1), channel_id=1, source_target_pairs={{4,0},{8,4},{12,8},{16,12},{20,16},{24,20},{28,24},{5,1},{9,5},{13... | collective-permute-start | bytes 2359304 | tf_op jit(solution)/shard_map/ppermute | solution.py:28
  2.7 10.3 %collective-permute-start = (f32[3,32,8,128]{3,2,1,0:T(8,128)S(1)}, f32[3,32,8,128]{3,2,1,0:T(8,128)S(1)}, u32[]{:S(2)}, u32[]{:S(2)}) collective-permute-start(f32[3,32,8,128]{3,2,1,0:T(8,128)S(1)} %get-tuple-element.16), channel_id=1, source_target_pairs={{1,2},{2,1},{5,6},{6,5},{9,10},{10,9},{13,14},{14,13},{17,18},{18,... | collective-permute-start | bytes 1179656 | tf_op jit(solution)/shard_map/ppermute | solution.py:31
  7.2 5.7 %collective-permute-start.1 = (f32[3,32,8,128]{3,2,1,0:T(8,128)S(1)}, f32[3,32,8,128]{3,2,1,0:T(8,128)S(1)}, u32[]{:S(2)}, u32[]{:S(2)}) collective-permute-start(f32[3,32,8,128]{3,2,1,0:T(8,128)S(1)} %get-tuple-element.17), channel_id=1, source_target_pairs={{0,1},{2,3},{1,0},{3,2},{4,5},{6,7},{5,4},{7,6},{8,9},{10,11},{9,8... | collective-permute-start | bytes 1179656 | tf_op jit(solution)/shard_map/ppermute | solution.py:31
  7.3 18.0 %collective-permute-start.4 = (f32[3,16,8,128]{3,2,1,0:T(8,128)S(1)}, f32[3,16,8,128]{3,2,1,0:T(8,128)S(1)}, u32[]{:S(2)}, u32[]{:S(2)}) collective-permute-start(f32[3,16,8,128]{3,2,1,0:T(8,128)S(1)} %get-tuple-element.19), channel_id=1, source_target_pairs={{5,2},{6,1},{9,6},{10,5},{13,10},{14,9},{17,14},{18,13},{21,18},{2... | collective-permute-start | bytes 589832 | tf_op jit(solution)/shard_map/ppermute | solution.py:38
  17.7 18.0 %collective-permute-start.2 = (f32[3,10,32,128]{3,2,1,0:T(8,128)S(1)}, f32[3,10,32,128]{3,2,1,0:T(8,128)S(1)}, u32[]{:S(2)}, u32[]{:S(2)}) collective-permute-start(f32[3,10,32,128]{3,2,1,0:T(8,128)S(1)} %pack_far.1), channel_id=1, source_target_pairs={{8,0},{12,4},{16,8},{20,12},{24,16},{28,20},{9,1},{13,5},{17,9},{2... | collective-permute-start | bytes 1474568 | tf_op jit(solution)/shard_map/ppermute | solution.py:28
  21.5 3.8 %collective-permute-start.5 = (f32[3,8,8,128]{3,2,1,0:T(8,128)S(1)}, f32[3,8,8,128]{3,2,1,0:T(8,128)S(1)}, u32[]{:S(2)}, u32[]{:S(2)}) collective-permute-start(f32[3,8,8,128]{3,2,1,0:T(8,128)S(1)} %get-tuple-element.20), channel_id=1, source_target_pairs={{0,1},{2,3},{1,0},{3,2},{4,5},{6,7},{5,4},{7,6},{8,9},{10,11},{9,8... | collective-permute-start | bytes 294920 | tf_op jit(solution)/shard_map/ppermute | solution.py:31
  23.6 1.7 %collective-permute-start.6 = (f32[3,8,8,128]{3,2,1,0:T(8,128)S(1)}, f32[3,8,8,128]{3,2,1,0:T(8,128)S(1)}, u32[]{:S(2)}, u32[]{:S(2)}) collective-permute-start(f32[3,8,8,128]{3,2,1,0:T(8,128)S(1)} %get-tuple-element.21), channel_id=1, source_target_pairs={{0,1},{2,3},{1,0},{3,2},{4,5},{6,7},{5,4},{7,6},{8,9},{10,11},{9,8... | collective-permute-start | bytes 294920 | tf_op jit(solution)/shard_map/ppermute | solution.py:31
